TPU v7x, 32 devices: a whole 2x2x4 slice. The times are simulated.
32 devices in a mesh: dp: 4 (over z), expert: 8 (over y, x, core).
Axes of the slice: x: 2, y: 2, z: 4, core: 2. Of those that a mesh axis runs over, the one named last changes fastest.
Arguments:
- queries: bfloat16 [4352, 1536], P(('dp', 'expert')), may hold values from -6 to 6
- fresh_keys: bfloat16 [4352, 256], P(('dp', 'expert')), may hold values from -1 to 1
- fresh_values: bfloat16 [4352, 256], P(('dp', 'expert')), may hold values from -6 to 6
- residual: bfloat16 [4352, 1536], P(('dp', 'expert')), may hold values from -6 to 6
- norm_gain: float32 [1536], replicated, may hold values from 0.25 to 1.75
- out_weight: bfloat16 [1536, 1536], replicated, may hold values from -0.15625 to 0.15625
- router_weight: bfloat16 [1536, 8], replicated, may hold values from -0.15625 to 0.15625
- gate_weight: bfloat16 [8, 1536, 384], P('expert'), may hold values from -0.15625 to 0.15625
- up_weight: bfloat16 [8, 1536, 384], P('expert'), may hold values from -0.15625 to 0.15625
- down_weight: bfloat16 [8, 384, 1536], P('expert'), may hold values from -0.3125 to 0.3125
- expert_ids: int32 [4352, 4], P(('dp', 'expert')), may hold values from 0 to 7, all different within a row; in each aligned block of 136 rows (0 to 135, 136 to 271, ...) at most 104 rows name the same one
- paged_keys: bfloat16 [384, 128, 256], P(('dp', 'expert')), may hold values from -1 to 1
- paged_values: bfloat16 [384, 128, 256], P(('dp', 'expert')), may hold values from -6 to 6
- decode_table: int32 [224, 4], P(('dp', 'expert')), may hold values from 0 to 11
- prefill_table: int32 [32, 4], P(('dp', 'expert')), may hold values from 0 to 11
- decode_len: int32 [32, 8], P(('dp', 'expert')), may hold values from 1 to 511, 2048 in all within a row
- prefill_len: int32 [32], P(('dp', 'expert')), may hold values from 0 to 512
- departing_keys: bfloat16 [32, 512, 256], P(('dp', 'expert')), may hold values from -1 to 1
- departing_values: bfloat16 [32, 512, 256], P(('dp', 'expert')), may hold values from -6 to 6
- destination: int32 [8, 4], P('expert'), may hold values from 0 to 3, each once within a row
Outputs:
- layer_out: bfloat16 [4352, 1536], P(('dp', 'expert'))
- moved_keys: bfloat16 [32, 512, 256], P(('dp', 'expert'))
- moved_values: bfloat16 [32, 512, 256], P(('dp', 'expert'))
Inputs may be any that keep to these rules, and one draw needn't show every extreme that they name: `expert_ids`: in each device's 136 rows no expert is named by more than 104 rows, a bound that some block reaches. `decode_len`: each device's 8 lengths sum to 2048 and the largest is 511. `destination`: each row is a permutation of the dp indices. `decode_table`: entries index pages of the device's own pool. `prefill_table`: entries index pages of the device's own pool.
All inputs are finite; a program needn't handle non-finite values.
Results may differ from a plain program's by a relative error of at most 0.0045.
Values may be sent and summed in bfloat16 or wider, within the bound.
A program may use at most 128 MiB of HBM per device.

v0:
```python
import jax
import jax.numpy as jnp
from jax import lax
from jax.sharding import PartitionSpec as P

QUERY_HEADS = 12
KEY_VALUE_HEADS = 2
HEAD_SIZE = 128
DEC_DEV = 8
PCH = 128
CONTEXT_LENGTH = 512


def attend(query_row_block, key_row_block, value_row_block, valid):
    batch_groups = query_row_block.shape[0]
    query_total = query_row_block.shape[1]
    key_total = key_row_block.shape[1]
    grouped_rows = query_row_block.reshape(
        batch_groups, query_total, KEY_VALUE_HEADS, QUERY_HEADS // KEY_VALUE_HEADS, HEAD_SIZE
    )
    key_head_rows = key_row_block.reshape(batch_groups, key_total, KEY_VALUE_HEADS, HEAD_SIZE)
    value_head_rows = value_row_block.reshape(batch_groups, key_total, KEY_VALUE_HEADS, HEAD_SIZE)
    scores = jnp.einsum(
        "bqhgd,bkhd->bqhgk", grouped_rows, key_head_rows, preferred_element_type=jnp.float32
    ) * HEAD_SIZE ** (-0.5)
    weights = jnp.where(valid[:, :, None, None, :], jnp.exp(scores), 0.0)
    totals = jnp.sum(weights, axis=-1)
    mixed = (
        jnp.einsum(
            "bqhgk,bkhd->bqhgd",
            weights.astype(jnp.bfloat16),
            value_head_rows,
            preferred_element_type=jnp.float32,
        )
        / totals[..., None]
    )
    return mixed.reshape(batch_groups, query_total, QUERY_HEADS * HEAD_SIZE).astype(jnp.bfloat16)


def capacity_for(token_count, route_count, expert_count):
    return min(token_count, (token_count * route_count // expert_count * 3 // 2 + 7) // 8 * 8)


def page_lookup(table, pool_flat):
    pool_count = pool_flat.shape[0]
    selector = (table[..., None] == jnp.arange(pool_count, dtype=jnp.int32)).astype(jnp.bfloat16)
    return jnp.einsum(
        "...p,pk->...k", selector, pool_flat, preferred_element_type=jnp.float32
    ).astype(jnp.bfloat16)


def on_device(
    queries,
    fresh_keys,
    fresh_values,
    residual,
    norm_gain,
    out_weight,
    router_weight,
    gate_weight,
    up_weight,
    down_weight,
    expert_ids,
    paged_keys,
    paged_values,
    decode_table,
    prefill_table,
    decode_len,
    prefill_len,
    departing_keys,
    departing_values,
    destination,
):
    width_total = KEY_VALUE_HEADS * HEAD_SIZE
    my_row = lax.axis_index("dp")
    target_row = destination[0]
    chosen = (target_row == my_row)[:, None, None]
    take_keys = jnp.sum(
        jnp.where(chosen, lax.all_gather(departing_keys, "dp", axis=0, tiled=True), 0),
        axis=0,
        keepdims=True,
    )
    take_values = jnp.sum(
        jnp.where(chosen, lax.all_gather(departing_values, "dp", axis=0, tiled=True), 0),
        axis=0,
        keepdims=True,
    )
    pool_count = paged_keys.shape[0]
    page_rows = paged_keys.shape[1]
    pool_key_flat = paged_keys.reshape(pool_count, page_rows * width_total)
    pool_value_flat = paged_values.reshape(pool_count, page_rows * width_total)
    resident_keys = page_lookup(decode_table, pool_key_flat).reshape(
        DEC_DEV - 1, CONTEXT_LENGTH, width_total
    )
    resident_values = page_lookup(decode_table, pool_value_flat).reshape(
        DEC_DEV - 1, CONTEXT_LENGTH, width_total
    )
    decode_keys = jnp.concatenate(
        [jnp.concatenate([resident_keys, take_keys], axis=0), fresh_keys[:DEC_DEV, None]], axis=1
    )
    decode_values = jnp.concatenate(
        [jnp.concatenate([resident_values, take_values], axis=0), fresh_values[:DEC_DEV, None]],
        axis=1,
    )
    positions = jnp.arange(CONTEXT_LENGTH, dtype=jnp.int32)
    decode_valid = jnp.concatenate(
        [positions[None, :] < decode_len[0][:, None], jnp.ones((DEC_DEV, 1), dtype=bool)], axis=1
    )[:, None, :]
    decode_out = attend(queries[:DEC_DEV, None], decode_keys, decode_values, decode_valid)[:, 0]
    context_keys = page_lookup(prefill_table[0], pool_key_flat).reshape(CONTEXT_LENGTH, width_total)
    context_values = page_lookup(prefill_table[0], pool_value_flat).reshape(
        CONTEXT_LENGTH, width_total
    )
    block_keys = jnp.concatenate([context_keys, fresh_keys[DEC_DEV:]], axis=0)[None]
    block_values = jnp.concatenate([context_values, fresh_values[DEC_DEV:]], axis=0)[None]
    block_pos = jnp.arange(PCH, dtype=jnp.int32)
    context_valid = jnp.broadcast_to(positions[None, :] < prefill_len[0], (PCH, CONTEXT_LENGTH))
    causal = block_pos[None, :] <= block_pos[:, None]
    block_valid = jnp.concatenate([context_valid, causal], axis=1)[None]
    block_out = attend(queries[DEC_DEV:][None], block_keys, block_values, block_valid)[0]
    attended = jnp.concatenate([decode_out, block_out], axis=0)
    hidden = residual.astype(jnp.float32) + jnp.dot(
        attended, out_weight, preferred_element_type=jnp.float32
    )
    variance = jnp.mean(hidden * hidden, axis=-1, keepdims=True)
    normed = (hidden * lax.rsqrt(variance + 1e-06) * norm_gain).astype(jnp.bfloat16)
    logits = jnp.dot(normed, router_weight, preferred_element_type=jnp.float32)
    expert_count = router_weight.shape[1]
    expert_range = jnp.arange(expert_count, dtype=jnp.int32)
    chosen = jnp.sum(
        jnp.where(expert_ids[:, :, None] == expert_range, logits[:, None, :], 0.0), axis=-1
    )
    chosen = jax.nn.sigmoid(chosen)
    gates = chosen / jnp.sum(chosen, axis=1, keepdims=True)
    token_count = expert_ids.shape[0]
    route_count = expert_ids.shape[1]
    capacity = capacity_for(token_count, route_count, expert_count)
    slot_total = expert_count * capacity
    flat_ids = expert_ids.reshape(-1)
    hits = (flat_ids[:, None] == expert_range[None, :]).astype(jnp.int32)
    ranks = jnp.sum((jnp.cumsum(hits, axis=0) - 1) * hits, axis=1)
    slot_of_route = flat_ids * capacity + ranks
    route_slots = (
        slot_of_route[:, None] == jnp.arange(slot_total, dtype=jnp.int32)[None, :]
    ).astype(jnp.bfloat16)
    token_slots = jnp.sum(route_slots.reshape(token_count, route_count, slot_total), axis=1)
    outgoing = jnp.einsum(
        "ts,td->sd", token_slots, normed, preferred_element_type=jnp.float32
    ).astype(jnp.bfloat16)
    outgoing = outgoing.reshape(expert_count, capacity, normed.shape[1])
    received = lax.all_to_all(outgoing, "expert", split_axis=0, concat_axis=0, tiled=True)
    gate_part = jnp.einsum(
        "scd,df->scf", received, gate_weight[0], preferred_element_type=jnp.float32
    )
    up_part = jnp.einsum("scd,df->scf", received, up_weight[0], preferred_element_type=jnp.float32)
    inner = (jax.nn.relu(gate_part) * up_part).astype(jnp.bfloat16)
    processed = jnp.einsum(
        "scf,fd->scd", inner, down_weight[0], preferred_element_type=jnp.float32
    ).astype(jnp.bfloat16)
    returned = lax.all_to_all(processed, "expert", split_axis=0, concat_axis=0, tiled=True)
    returned_flat = returned.reshape(slot_total, returned.shape[2])
    route_out = jnp.dot(route_slots, returned_flat, preferred_element_type=jnp.float32).astype(
        jnp.bfloat16
    )
    route_out = route_out.reshape(token_count, route_count, -1)
    mixture = jnp.sum(gates[:, :, None] * route_out.astype(jnp.float32), axis=1)
    layer_out = (hidden + mixture).astype(jnp.bfloat16)
    last_len = decode_len[0, DEC_DEV - 1]
    moved_keys = lax.dynamic_update_slice(
        take_keys,
        fresh_keys[DEC_DEV - 1][None, None],
        (jnp.zeros((), jnp.int32), last_len, jnp.zeros((), jnp.int32)),
    )
    moved_values = lax.dynamic_update_slice(
        take_values,
        fresh_values[DEC_DEV - 1][None, None],
        (jnp.zeros((), jnp.int32), last_len, jnp.zeros((), jnp.int32)),
    )
    return (layer_out, moved_keys, moved_values)


def solution(mesh):
    return jax.shard_map(
        on_device,
        mesh=mesh,
        in_specs=(
            P(("dp", "expert"), None),
            P(("dp", "expert"), None),
            P(("dp", "expert"), None),
            P(("dp", "expert"), None),
            P(),
            P(),
            P(),
            P("expert", None, None),
            P("expert", None, None),
            P("expert", None, None),
            P(("dp", "expert"), None),
            P(("dp", "expert"), None, None),
            P(("dp", "expert"), None, None),
            P(("dp", "expert"), None),
            P(("dp", "expert"), None),
            P(("dp", "expert"), None),
            P(("dp", "expert")),
            P(("dp", "expert"), None, None),
            P(("dp", "expert"), None, None),
            P("expert", None),
        ),
        out_specs=(
            P(("dp", "expert"), None),
            P(("dp", "expert"), None, None),
            P(("dp", "expert"), None, None),
        ),
        check_vma=False,
    )
```

profile of v0, /device:TPU:0, one launch (start us, length us, event | category | flops | bytes accessed | tf_op | source)
XLA Modules:
  0.0 188.1 jit_solution(14105094751354102917)
XLA Ops:
  9.3 1.6 reshape.234
  10.9 2.4 %reshape.233 = bf16[12,32768,1]{1,0,2:T(8,128)(2,1)} reshape(bf16[12,128,256]{2,1,0:T(8,128)(2,1)} %param.32) | data formatting | bytes 1572864 | tf_op jit(solution)/shard_map/reshape | solution.py:91
  13.4 1.3 pad.20
  15.4 2.1 %convolution_convert_fusion = bf16[7,4,32768]{2,0,1:T(8,128)(2,1)} fusion(bf16[12,32768,1]{1,0,2:T(8,128)(2,1)S(1)} %reshape.234, s32[7,4]{0,1:T(4,128)S(1)} %copy-done.20), kind=kOutput, calls=%fused_computation | convolution fusion | flops 22937936 | bytes 2621552 | tf_op jit(solution)/shard_map/...p,pk->...k/dot_general | solution.py:47
  21.7 1.1 convolution_convert_fusion.3
  23.0 1.4 reduce-window.6
  25.6 4.4 %copy.148 = bf16[7,4,32768]{2,1,0:T(4,128)(2,1)} copy(bf16[7,4,32768]{2,0,1:T(8,128)(2,1)} %convolution_convert_fusion) | data formatting | bytes 3670016 | tf_op jit(solution)/shard_map/convert_element_type | solution.py:49
  30.0 5.5 %concatenate.54 = bf16[7,512,2,128]{3,2,1,0:T(2,128)(2,1)} reshape(bf16[7,4,32768]{2,1,0:T(4,128)(2,1)} %copy.148) | data formatting | bytes 3670016 | tf_op jit(solution)/shard_map/concatenate | solution.py:99
  35.5 3.1 %copy.150 = bf16[7,512,2,128]{3,1,2,0:T(8,128)(2,1)} copy(bf16[7,512,2,128]{3,2,1,0:T(2,128)(2,1)} %concatenate.54) | data formatting | bytes 3670016 | tf_op jit(solution)/shard_map/concatenate | solution.py:99
  39.2 2.8 %copy.143 = bf16[7,4,32768]{2,1,0:T(4,128)(2,1)} copy(bf16[7,4,32768]{2,0,1:T(8,128)(2,1)S(1)} %convolution_convert_fusion.1) | data formatting | bytes 3670016 | tf_op jit(solution)/shard_map/convert_element_type | solution.py:49
  42.0 4.8 %concatenate.49 = bf16[7,512,2,128]{3,2,1,0:T(2,128)(2,1)S(1)} reshape(bf16[7,4,32768]{2,1,0:T(4,128)(2,1)} %copy.143) | data formatting | bytes 3670016 | tf_op jit(solution)/shard_map/concatenate | solution.py:102
  46.8 1.6 copy.145
  49.1 1.2 concatenate.62
  50.9 1.2 concatenate.58
  54.7 1.6 fusion.59
  56.3 13.0 %all-gather.5.cloned.1.call-done = bf16[4,512,256]{2,1,0:T(8,128)(2,1)} async-done(((bf16[1,512,256]{2,1,0:T(8,128)(2,1)}), bf16[4,512,256]{2,1,0:T(8,128)(2,1)}) %all-gather.5.cloned.1.call-update) | async-done | bytes 1048592 | tf_op jit(solution)/shard_map/all_gather | solution.py:79
  69.3 3.0 %select_reduce_fusion = (bf16[512,256]{1,0:T(8,128)(2,1)}, bf16[512,256]{1,0:T(8,128)(2,1)}) fusion(bf16[4,512,256]{2,1,0:T(8,128)(2,1)} %all-gather.5.cloned.1.call-done, pred[4]{0:T(512)(128)(4,1)S(1)} %compare_bitcast_fusion, bf16[4,512,256]{2,1,0:T(8,128)(2,1)} %all-gather.3.cloned.1.call-done), kind=kLoop, calls=%fused_computation.49 | loop fusion | flops 1835008 | bytes 2621444 | tf_op jit(solution)/shard_map/reduce_sum | solution.py:78
  72.3 1.1 copy.149
  74.2 1.1 copy.144
  76.2 1.9 fusion.91
  79.1 3.5 %multiply_reduce_fusion.1 = (f32[136]{0:T(256)S(1)}, f32[136,1536]{1,0:T(8,128)S(1)}) fusion(bf16[1536,1536]{1,0:T(8,128)(2,1)} %param.25, bf16[128,1536]{0,1:T(8,128)(2,1)} %bitcast.154, bf16[8,1536]{0,1:T(8,128)(2,1)S(1)} %bitcast.146, bf16[136,1536]{1,0:T(8,128)(2,1)S(1)} %copy-done.26), kind=kOutput, calls=%fused_computation.57 | convolution fusion | flops 643399552 | bytes 6390304 | tf_op jit(solution)/shard_map/dot_general | solution.py:122
  83.5 35.1 %all_to_all.10 = bf16[8,104,1536]{2,1,0:T(8,128)(2,1)S(1)} all-to-all(bf16[8,104,1536]{2,1,0:T(8,128)(2,1)S(1)} %bitcast.135), channel_id=1, replica_groups=mesh['dp'=4,'expert'=8] {'expert'}, dimensions={0} | all-to-all | bytes 5111808 | tf_op jit(solution)/shard_map/all_to_all | solution.py:151
  118.6 1.5 copy-done.3
  120.1 2.6 %convolution_maximum_fusion = f32[8,104,384]{2,1,0:T(8,128)} fusion(bf16[8,104,1536]{2,1,0:T(8,128)(2,1)S(1)} %all_to_all.10, bf16[1,1536,384]{2,1,0:T(8,128)(2,1)S(1)} %copy-done.25), kind=kOutput, calls=%fused_computation.34 | convolution fusion | flops 981786624 | bytes 5013504 | tf_op jit(solution)/shard_map/scd,df->scf/dot_general | solution.py:152
  122.7 6.8 %convolution_convert_fusion.4 = bf16[8,104,1536]{2,1,0:T(8,128)(2,1)} fusion(bf16[1,384,1536]{2,1,0:T(8,128)(2,1)S(1)} %copy-done, f32[8,104,384]{2,1,0:T(8,128)} %convolution_maximum_fusion, bf16[8,104,1536]{2,1,0:T(8,128)(2,1)} %copy-done.3, bf16[1,1536,384]{2,1,0:T(8,128)(2,1)} %param.28), kind=kOutput, calls=%fused_computation.5 | convolution fusion | flops 1964851200 | bytes 8749056 | tf_op jit(solution)/shard_map/scf,fd->scd/dot_general | solution.py:157
  129.5 4.8 %all-to-all-start.1 = ((bf16[8,104,1536]{2,1,0:T(8,128)(2,1)}), bf16[8,104,1536]{2,1,0:T(8,128)(2,1)}, u32[]{:S(2)}, u32[]{:S(2)}) async-start(bf16[8,104,1536]{2,1,0:T(8,128)(2,1)} %convolution_convert_fusion.4), calls=%async_computation.1 | async-start | bytes 5111808 | tf_op jit(solution)/shard_map/all_to_all | solution.py:160
  137.4 1.3 dynamic_update_slice.6
  138.7 1.3 dynamic_update_slice.7
  140.0 25.7 %all-to-all-done.1 = bf16[8,104,1536]{2,1,0:T(8,128)(2,1)} async-done(((bf16[8,104,1536]{2,1,0:T(8,128)(2,1)}), bf16[8,104,1536]{2,1,0:T(8,128)(2,1)}, u32[]{:S(2)}, u32[]{:S(2)}) %all-to-all-start.1) | async-done | bytes 2555936 | tf_op jit(solution)/shard_map/all_to_all | solution.py:160
  165.7 5.4 %fusion.2 = f32[544,1536]{1,0:T(8,128)} fusion(bf16[832,1536]{1,0:T(8,128)(2,1)} %bitcast.41, s32[544]{0:T(1024)S(1)} %multiply_add_fusion.1), kind=kOutput, calls=%fused_computation.11 | convolution fusion | flops 1392535552 | bytes 5900416 | tf_op jit(solution)/shard_map/dot_general | solution.py:162
  171.0 5.0 %reshape.232 = f32[136,4,1536]{2,1,0:T(4,128)} reshape(f32[544,1536]{1,0:T(8,128)} %fusion.2) | data formatting | bytes 6684672 | tf_op jit(solution)/shard_map/convert_element_type | solution.py:166
  176.0 4.4 %multiply_reduce_fusion = f32[136,1536]{1,0:T(8,128)S(1)} fusion(f32[136,4,1536]{2,1,0:T(4,128)} %reshape.232, f32[136,4]{1,0:T(8,128)S(1)} %copy.163), kind=kLoop, calls=%fused_computation.7 | loop fusion | flops 1462272 | bytes 4180096 | tf_op jit(solution)/shard_map/reduce_sum | solution.py:166
  (121 shorter events, 17.5 us)
Async XLA Ops:
  7.2 115.6 %copy-start = (bf16[1,384,1536]{2,1,0:T(8,128)(2,1)S(1)}, bf16[1,384,1536]{2,1,0:T(8,128)(2,1)}, u32[]{:S(2)}) copy-start(bf16[1,384,1536]{2,1,0:T(8,128)(2,1)} %param.29) | copy-start | bytes 3538948
  7.2 6.1 %copy-start.2 = (bf16[12,128,256]{2,1,0:T(8,128)(2,1)S(1)}, bf16[12,128,256]{2,1,0:T(8,128)(2,1)}, u32[]{:S(2)}) copy-start(bf16[12,128,256]{2,1,0:T(8,128)(2,1)} %param.31) | copy-start | bytes 2359300
  7.2 49.1 %all-gather.3.cloned.1.call-start = ((), (), s32[]{:S(2)}) async-start(), calls=%async_computation.2 | async-start | bytes 1310720 | tf_op jit(solution)/shard_map/all_gather | solution.py:84
  7.9 61.4 %all-gather.5.cloned.1.call-start = ((), (), s32[]{:S(2)}) async-start(), calls=%async_computation.3 | async-start | bytes 1310720 | tf_op jit(solution)/shard_map/all_gather | solution.py:79
  10.9 3.8 %copy-start.9 = (bf16[136,256]{1,0:T(8,128)(2,1)S(1)}, bf16[136,256]{1,0:T(8,128)(2,1)}, u32[]{:S(2)}) copy-start(bf16[136,256]{1,0:T(8,128)(2,1)} %param.21) | copy-start | bytes 208900
  10.9 3.8 %copy-start.22 = (s32[1,8]{1,0:T(1,128)S(1)}, s32[1,8]{1,0:T(1,128)}, u32[]{:S(2)}) copy-start(s32[1,8]{1,0:T(1,128)} %param.35) | copy-start | bytes 100
  10.9 4.5 %copy-start.20 = (s32[7,4]{0,1:T(4,128)S(1)}, s32[7,4]{0,1:T(4,128)}, u32[]{:S(2)}) copy-start(s32[7,4]{0,1:T(4,128)} %param.33) | copy-start | bytes 340
  13.3 4.1 %copy-start.1 = (bf16[12,32768,1]{1,0,2:T(8,128)(2,1)S(1)}, bf16[12,32768,1]{1,0,2:T(8,128)(2,1)}, u32[]{:S(2)}) copy-start(bf16[12,32768,1]{1,0,2:T(8,128)(2,1)} %reshape.233) | copy-start | bytes 2359300
  15.4 2.8 %copy-start.7 = (bf16[136,256]{1,0:T(8,128)(2,1)S(1)}, bf16[136,256]{1,0:T(8,128)(2,1)}, u32[]{:S(2)}) copy-start(bf16[136,256]{1,0:T(8,128)(2,1)} %param.22) | copy-start | bytes 208900
  18.2 2.5 %copy-start.21 = (s32[1,4]{1,0:T(1,128)S(1)}, s32[1,4]{1,0:T(1,128)}, u32[]{:S(2)}) copy-start(s32[1,4]{1,0:T(1,128)} %param.34) | copy-start | bytes 52
  19.4 3.4 %copy-start.12 = (s32[136,4]{0,1:T(4,128)S(1)}, s32[136,4]{0,1:T(4,128)}, u32[]{:S(2)}) copy-start(s32[136,4]{0,1:T(4,128)} %param.30) | copy-start | bytes 6532
  46.8 3.6 %slice-start.1 = ((bf16[136,1536]{1,0:T(8,128)(2,1)}), bf16[128,1536]{1,0:T(8,128)(2,1)S(1)}, s32[]{:S(2)}) async-start(bf16[136,1536]{1,0:T(8,128)(2,1)} %param.20), calls=%async_computation.5 | async-start | bytes 786432 | tf_op jit(solution)/shard_map/slice | solution.py:120
  46.8 3.8 %slice-start.3 = ((bf16[136,256]{1,0:T(8,128)(2,1)}), bf16[128,256]{1,0:T(8,128)(2,1)S(1)}, s32[]{:S(2)}) async-start(bf16[136,256]{1,0:T(8,128)(2,1)} %param.21), calls=%async_computation.7 | async-start | bytes 131072 | tf_op jit(solution)/shard_map/slice | solution.py:114
  46.8 5.5 %slice-start.2 = ((bf16[136,256]{1,0:T(8,128)(2,1)}), bf16[128,256]{1,0:T(8,128)(2,1)S(1)}, s32[]{:S(2)}) async-start(bf16[136,256]{1,0:T(8,128)(2,1)} %param.22), calls=%async_computation.6 | async-start | bytes 131072 | tf_op jit(solution)/shard_map/slice | solution.py:115
  48.5 4.1 %copy-start.18 = (pred[8,512]{1,0:T(8,128)(4,1)S(1)}, pred[8,512]{1,0:T(8,128)(4,1)}, u32[]{:S(2)}) copy-start(pred[8,512]{1,0:T(8,128)(4,1)} %iota_compare_fusion.7) | copy-start | bytes 12292
  48.5 4.8 %copy-start.24 = (pred[512]{0:T(512)(128)(4,1)S(1)}, pred[512]{0:T(512)(128)(4,1)}, u32[]{:S(2)}) copy-start(pred[512]{0:T(512)(128)(4,1)} %iota_compare_fusion.11) | copy-start | bytes 1540
  48.5 4.8 %copy-start.13 = (s32[136,4]{0,1:T(4,128)S(1)}, s32[136,4]{0,1:T(4,128)}, u32[]{:S(2)}) copy-start(s32[136,4]{0,1:T(4,128)} %param.30) | copy-start | bytes 6532
  48.5 5.1 %copy-start.27 = (s32[1,4]{1,0:T(1,128)S(1)}, s32[1,4]{1,0:T(1,128)}, u32[]{:S(2)}) copy-start(s32[1,4]{1,0:T(1,128)} %param.39) | copy-start | bytes 52
  48.5 5.1 %copy-start.11 = (pred[128,128]{0,1:T(8,128)(4,1)S(1)}, pred[128,128]{0,1:T(8,128)(4,1)}, u32[]{:S(2)}) copy-start(pred[128,128]{0,1:T(8,128)(4,1)} %iota_compare_fusion.3) | copy-start | bytes 49156
  56.3 19.9 %copy-start.4 = (bf16[7,512,2,128]{3,1,2,0:T(8,128)(2,1)S(1)}, bf16[7,512,2,128]{3,1,2,0:T(8,128)(2,1)}, u32[]{:S(2)}) copy-start(bf16[7,512,2,128]{3,1,2,0:T(8,128)(2,1)} %copy.150) | copy-start | bytes 5505028
  56.3 19.9 %slice-start = ((bf16[136,1536]{1,0:T(8,128)(2,1)}), bf16[8,1536]{1,0:T(8,128)(2,1)S(1)}, s32[]{:S(2)}) async-start(bf16[136,1536]{1,0:T(8,128)(2,1)} %param.20), calls=%async_computation.4 | async-start | bytes 49152 | tf_op jit(solution)/shard_map/slice | solution.py:109
  76.2 1.9 %copy-start.5 = (bf16[7,512,2,128]{3,1,2,0:T(8,128)(2,1)S(1)}, bf16[7,512,2,128]{3,1,2,0:T(8,128)(2,1)}, u32[]{:S(2)}) copy-start(bf16[7,512,2,128]{3,1,2,0:T(8,128)(2,1)} %copy.145) | copy-start | bytes 5505028
  76.2 1.9 %copy-start.6 = (bf16[1,512,2,128]{3,1,2,0:T(8,128)(2,1)S(1)}, bf16[1,512,2,128]{3,1,2,0:T(8,128)(2,1)}, u32[]{:S(2)}) copy-start(bf16[1,512,2,128]{3,1,2,0:T(8,128)(2,1)} %copy.146) | copy-start | bytes 786436
  76.2 1.9 %copy-start.19 = (bf16[8,1,2,128]{3,1,2,0:T(2,128)(2,1)S(1)}, bf16[8,1,2,128]{3,1,2,0:T(2,128)(2,1)}, u32[]{:S(2)}) copy-start(bf16[8,1,2,128]{3,1,2,0:T(2,128)(2,1)} %copy.147) | copy-start | bytes 12292
  79.1 3.5 %copy-start.15 = (f32[1536]{0:T(1024)S(1)}, f32[1536]{0:T(1024)}, u32[]{:S(2)}) copy-start(f32[1536]{0:T(1024)} %param.24) | copy-start | bytes 18436
  83.5 36.6 %copy-start.25 = (bf16[1,1536,384]{2,1,0:T(8,128)(2,1)S(1)}, bf16[1,1536,384]{2,1,0:T(8,128)(2,1)}, u32[]{:S(2)}) copy-start(bf16[1,1536,384]{2,1,0:T(8,128)(2,1)} %param.27) | copy-start | bytes 3538948
  129.5 4.8 %copy-start.23 = (s32[1,8]{1,0:T(1,128)S(1)}, s32[1,8]{1,0:T(1,128)}, u32[]{:S(2)}) copy-start(s32[1,8]{1,0:T(1,128)} %param.35) | copy-start | bytes 100
  129.5 7.3 %copy-start.10 = (bf16[136,256]{1,0:T(8,128)(2,1)S(1)}, bf16[136,256]{1,0:T(8,128)(2,1)}, u32[]{:S(2)}) copy-start(bf16[136,256]{1,0:T(8,128)(2,1)} %param.21) | copy-start | bytes 208900
  129.5 7.4 %copy-start.8 = (bf16[136,256]{1,0:T(8,128)(2,1)S(1)}, bf16[136,256]{1,0:T(8,128)(2,1)}, u32[]{:S(2)}) copy-start(bf16[136,256]{1,0:T(8,128)(2,1)} %param.22) | copy-start | bytes 208900
  129.5 7.4 %copy-start.16 = (bf16[1536,8]{0,1:T(8,128)(2,1)S(1)}, bf16[1536,8]{0,1:T(8,128)(2,1)}, u32[]{:S(2)}) copy-start(bf16[1536,8]{0,1:T(8,128)(2,1)} %param.26) | copy-start | bytes 73732
  129.5 7.7 %copy-start.14 = (s32[136,4]{0,1:T(4,128)S(1)}, s32[136,4]{0,1:T(4,128)}, u32[]{:S(2)}) copy-start(s32[136,4]{0,1:T(4,128)} %param.30) | copy-start | bytes 6532
  129.5 36.1 %all-to-all-start.1 = ((bf16[8,104,1536]{2,1,0:T(8,128)(2,1)}), bf16[8,104,1536]{2,1,0:T(8,128)(2,1)}, u32[]{:S(2)}, u32[]{:S(2)}) async-start(bf16[8,104,1536]{2,1,0:T(8,128)(2,1)} %convolution_convert_fusion.4), calls=%async_computation.1 | async-start | bytes 5111808 | tf_op jit(solution)/shard_map/all_to_all | solution.py:160
  (3 other events, 4.2 us)
Sparse Core Ops, SparseCore 0:
  9.6 30.6 all-gather.2
  41.8 27.4 all-gather.4
where the time goes:
time: 189 us; the launch traced here: 188 us
  local copies, waits for them, and re-layouts  49.4 us (26%)
  waiting for transfers between devices  40.1 us (21%)
  blocking collectives  35.1 us (19%)
  matrix products  29.1 us (15%)
  between operations  17.2 us (9%)
  other arithmetic  12.3 us (7%)
  starting transfers between devices  4.84 us (3%)
    all_to_all x1, blocking collectives, on_device(): lax.all_to_all(outgoing, 'expert', split_axis=0, concat_axis=0, tiled=True)  35.1 us
    all_to_all x1, waiting for transfers between devices, on_device(): lax.all_to_all(processed, 'expert', split_axis=0, concat_axis=0, tiled=True)  25.7 us
    all_gather x1, waiting for transfers between devices, on_device(): lax.all_gather(departing_keys, 'dp', axis=0, tiled=True)  13 us
    concatenate x2, local copies, waits for them, and re-layouts, on_device(): jnp.concatenate([resident_keys, take_keys], axis=0)  8.59 us
    convert_element_type x2, local copies, waits for them, and re-layouts, page_lookup(): return jnp.einsum('...p,pk->...k', selector, pool_flat, preferred_element...  7.23 us
    dot_general x1, matrix products, on_device(): jnp.einsum('scf,fd->scd', inner, down_weight[0], preferred_element_type=j...  6.75 us
    concatenate x2, local copies, waits for them, and re-layouts, on_device(): jnp.concatenate([resident_values, take_values], axis=0)  6.41 us
    dot_general x1, matrix products, on_device(): jnp.dot(route_slots, returned_flat, preferred_element_type=jnp.float32)  5.36 us
  transfers between devices with their start and end apart: 3, of which 2 were waited for; matrix products, arithmetic and copies ran while one was open for 27% of the time, Pallas kernels for 0%

commit v1 on v0

v1 whole, which is shorter than its diff:
```python
import functools

import jax
import jax.numpy as jnp
from jax import lax
from jax.experimental import pallas as pl
from jax.experimental.pallas import tpu as pltpu
from jax.sharding import PartitionSpec as P

QUERY_HEADS = 12
KEY_VALUE_HEADS = 2
GROUP = QUERY_HEADS // KEY_VALUE_HEADS
HEAD = 128
DEC = 8
SCALE = HEAD ** (-0.5)
MESH = pl.DeviceIdType.MESH
F32 = jnp.float32
BF16 = jnp.bfloat16
NT = (((1,), (1,)), ((), ()))


def iota(shape, dim):
    return lax.broadcasted_iota(jnp.int32, shape, dim)


def kernel(
    n_dp, n_ex,
    dec_table, pre_table, dec_len, pre_len, destination,
    queries, fresh_k, fresh_v, residual, gain, router, ids, pool_k, pool_v, dep_k, dep_v,
    out_w, gate_w, up_w, down_w,
    layer_out, moved_k, moved_v,
    wo, wg, wu, wd, hidden, attended, masks, tokens, partial, inbox,
    ask, answer, asked, answered, got_k, got_v,
    w_sem, ask_s, ask_r, ans_s, ans_r, mk_s, mk_r, mv_s, mv_r, msk_s, msk_r, g_s, g_r, r_s, r_r,
):
    row = lax.axis_index("dp")
    me = lax.axis_index("expert")
    count = queries.shape[0]
    padded = tokens.shape[1]
    cut = (padded // 2 + 15) // 16 * 16
    spans = ((0, cut), (cut, padded - cut))
    pool_pages, page = pool_k.shape[0], pool_k.shape[1]
    context = dep_k.shape[1]
    steps = n_ex.bit_length() - 1
    bits = [1 << b for b in range(steps)]
    orders = (bits[1:] + bits[:1], bits[1:][::-1] + bits[:1])

    weights = [
        pltpu.make_async_copy(src, dst, w_sem.at[i])
        for i, (src, dst) in enumerate(((out_w, wo), (gate_w.at[0], wg), (up_w.at[0], wu), (down_w.at[0], wd)))
    ]
    for copy in weights:
        copy.start()

    barrier = pltpu.get_barrier_semaphore()
    for d in range(1, n_dp):
        pl.semaphore_signal(barrier, inc=1, device_id={"dp": (row + d) % n_dp}, device_id_type=MESH)
    for d in range(1, n_ex):
        pl.semaphore_signal(barrier, inc=1, device_id={"expert": (me + d) % n_ex}, device_id_type=MESH)
    pl.semaphore_wait(barrier, n_dp + n_ex - 2)

    last = queries[0:16, :].astype(F32)[DEC - 1:DEC, :]
    line = iota((16, HEAD), 0)
    message = jnp.zeros((16, HEAD), F32)
    for h in range(QUERY_HEADS):
        message = jnp.where(line == h, last[:, h * HEAD:(h + 1) * HEAD], message)
    last_len = dec_len[0, DEC - 1]
    message = jnp.where(line == QUERY_HEADS, (last_len // 16).astype(F32), message)
    message = jnp.where(line == QUERY_HEADS + 1, (last_len % 16).astype(F32), message)
    ask[...] = message.astype(BF16)
    asked[row] = message.astype(BF16)

    def to_row(src, dst, send, recv, d):
        return pltpu.make_async_remote_copy(
            src_ref=src, dst_ref=dst.at[row], send_sem=send.at[d], recv_sem=recv.at[d],
            device_id={"dp": (row + d) % n_dp}, device_id_type=MESH)

    def from_row(src, dst, send, recv, d):
        return pltpu.make_async_remote_copy(
            src_ref=src, dst_ref=dst.at[(row + n_dp - d) % n_dp], send_sem=send.at[d], recv_sem=recv.at[d],
            device_id={"dp": (row + d) % n_dp}, device_id_type=MESH)

    for d in range(1, n_dp):
        to_row(ask, asked, ask_s, ask_r, d).start()

    chose = jnp.zeros((count, HEAD), F32)
    lane = iota((count, HEAD), 1)
    for k in range(ids.shape[1]):
        chose = jnp.where(ids[:, k:k + 1] == lane, 1.0, chose)
    masks[me] = jnp.concatenate([chose, jnp.zeros((padded - count, HEAD), F32)], axis=0).astype(BF16)

    def mask_copy(d, slot):
        return pltpu.make_async_remote_copy(
            src_ref=masks.at[slot], dst_ref=masks.at[slot], send_sem=msk_s.at[d], recv_sem=msk_r.at[d],
            device_id={"expert": (me + d) % n_ex}, device_id_type=MESH)

    for d in range(1, n_ex):
        mask_copy(d, me).start()

    for d in range(1, n_dp):
        to_row(dep_k.at[0], got_k, mk_s, mk_r, d).start()
        to_row(dep_v.at[0], got_v, mv_s, mv_r, d).start()
    got_k[row] = dep_k[0]
    got_v[row] = dep_v[0]

    small = iota((16, page), 0)
    spot = iota((16, page), 1)
    lens = jnp.zeros((16, page), jnp.int32)
    tables = [jnp.full((16, page), -1, jnp.int32) for _ in range(dec_table.shape[1])]
    for s in range(DEC - 1):
        lens = jnp.where(small == s, dec_len[0, s], lens)
        for p in range(len(tables)):
            tables[p] = jnp.where(small == s, dec_table[s, p], tables[p])
    pieces = []
    for g in range(pool_pages):
        piece = jnp.zeros((16, page), F32)
        for p, table in enumerate(tables):
            piece += jnp.where((table == g) & (spot + p * page < lens), 1.0, 0.0)
        pieces.append(piece)
    times = jnp.concatenate(pieces, axis=1)
    times = jnp.concatenate([times] * GROUP, axis=0)

    def decode_part(kh):
        cols = slice(kh * HEAD, (kh + 1) * HEAD)
        q = jnp.concatenate(
            [queries[0:16, (kh * GROUP + g) * HEAD:(kh * GROUP + g + 1) * HEAD] for g in range(GROUP)], axis=0)
        keys = pool_k[:, :, cols].reshape(pool_pages * page, HEAD)
        values = pool_v[:, :, cols].reshape(pool_pages * page, HEAD)
        s = lax.dot_general(q, keys, NT, preferred_element_type=F32) * SCALE
        w = jnp.exp(s) * times
        return jnp.dot(w.astype(BF16), values, preferred_element_type=F32), jnp.sum(w, axis=1, keepdims=True)

    decoded = [decode_part(kh) for kh in range(KEY_VALUE_HEADS)]

    for d in range(1, n_dp):
        from_row(ask, asked, ask_s, ask_r, d).wait_recv()
    q = asked[...].reshape(n_dp * 16, HEAD)
    meta = asked[...].astype(F32)
    limits = meta[:, QUERY_HEADS:QUERY_HEADS + 1, 0:1] * 16.0 + meta[:, QUERY_HEADS + 1:QUERY_HEADS + 2, 0:1]
    limits = jnp.broadcast_to(limits, (n_dp, 16, 1)).reshape(n_dp * 16, 1)
    live = iota((n_dp * 16, context), 1).astype(F32) < limits
    head_line = iota((n_dp * 16, 1), 0) % 16
    sums, totals = None, None
    for kh in range(KEY_VALUE_HEADS):
        cols = slice(kh * HEAD, (kh + 1) * HEAD)
        s = lax.dot_general(q, dep_k[0, :, cols], NT, preferred_element_type=F32) * SCALE
        mine = (head_line >= kh * GROUP) & (head_line < (kh + 1) * GROUP)
        w = jnp.where(live & mine, jnp.exp(s), 0.0)
        mixed = jnp.dot(w.astype(BF16), dep_v[0, :, cols], preferred_element_type=F32)
        total = jnp.sum(w, axis=1, keepdims=True)
        sums = mixed if sums is None else sums + mixed
        totals = total if totals is None else totals + total
    answer[:, 0:16, :] = sums.reshape(n_dp, 16, HEAD)
    answer[:, 16:32, :] = jnp.broadcast_to(totals, (n_dp * 16, HEAD)).reshape(n_dp, 16, HEAD)
    answered[row] = answer[row]

    def reply(d, slot):
        return pltpu.make_async_remote_copy(
            src_ref=answer.at[(row + d) % n_dp], dst_ref=answered.at[slot],
            send_sem=ans_s.at[d], recv_sem=ans_r.at[d],
            device_id={"dp": (row + d) % n_dp}, device_id_type=MESH)

    for d in range(1, n_dp):
        reply(d, row).start()

    r = iota((count, context), 0)
    c = iota((count, context), 1)
    context_valid = (r >= DEC) & (c < pre_len[0])
    r = iota((count, count), 0)
    c = iota((count, count), 1)
    fresh_valid = (c <= r) & ((c >= DEC) | (c == r))
    fresh_parts = []
    for kh in range(KEY_VALUE_HEADS):
        cols = slice(kh * HEAD, (kh + 1) * HEAD)
        picks = [pre_table[0, p] for p in range(pre_table.shape[1])]
        keys = jnp.concatenate([pool_k[p, :, cols] for p in picks], axis=0)
        values = jnp.concatenate([pool_v[p, :, cols] for p in picks], axis=0)
        for g in range(GROUP):
            h = kh * GROUP + g
            q = queries[:, h * HEAD:(h + 1) * HEAD]
            s = lax.dot_general(q, keys, NT, preferred_element_type=F32) * SCALE
            w = jnp.where(context_valid, jnp.exp(s), 0.0)
            s = lax.dot_general(q, fresh_k[:, cols], NT, preferred_element_type=F32) * SCALE
            wf = jnp.where(fresh_valid, jnp.exp(s), 0.0)
            total = jnp.sum(w, axis=1, keepdims=True) + jnp.sum(wf, axis=1, keepdims=True)
            mixed = jnp.dot(w.astype(BF16), values, preferred_element_type=F32)
            mixed += jnp.dot(wf.astype(BF16), fresh_v[:, cols], preferred_element_type=F32)
            part, part_total = decoded[kh]
            fresh_parts.append((
                mixed[0:DEC] + part[g * 16:g * 16 + DEC],
                total[0:DEC] + part_total[g * 16:g * 16 + DEC],
            ))
            attended[DEC:count, h * HEAD:(h + 1) * HEAD] = mixed[DEC:] / total[DEC:]

    for d in range(1, n_dp):
        reply(d, (row + n_dp - d) % n_dp).wait_recv()
    arrived = jnp.zeros((32, HEAD), F32)
    for i in range(n_dp):
        arrived = jnp.where(destination[0, i] == row, answered[i], arrived)
    seventh = iota((DEC, HEAD), 0) == DEC - 1
    for h in range(QUERY_HEADS):
        mixed, total = fresh_parts[h]
        mixed = mixed + jnp.where(seventh, arrived[h:h + 1, :], 0.0)
        total = total + jnp.where(seventh, arrived[16 + h:17 + h, :], 0.0)
        attended[0:DEC, h * HEAD:(h + 1) * HEAD] = mixed / total

    weights[0].wait()
    x = residual[...].astype(F32) + jnp.dot(attended[...].astype(BF16), wo[...], preferred_element_type=F32)
    hidden[...] = x
    variance = jnp.mean(x * x, axis=-1, keepdims=True)
    normed = x * lax.rsqrt(variance + 1e-06) * gain[...]
    tokens[me] = jnp.concatenate([normed, jnp.zeros((padded - count, x.shape[1]), F32)], axis=0).astype(BF16)

    def flip(index, flips):
        for b in flips:
            index = index + b - 2 * b * ((index // b) % 2)
        return index

    def place(half, flips):
        return sum(1 << orders[half].index(b) for b in flips)

    def flips_of(half, subset):
        return [orders[half][k] for k in range(steps) if subset >> k & 1]

    def gather_copy(half, subset, k, arriving):
        start, size = spans[half]
        owner = flip(me, flips_of(half, subset + (1 << k) if arriving else subset))
        block = tokens.at[owner, pl.ds(start, size)]
        sem = half * n_ex + (1 << k) + subset
        return pltpu.make_async_remote_copy(
            src_ref=block, dst_ref=block, send_sem=g_s.at[sem], recv_sem=g_r.at[sem],
            device_id={"expert": flip(me, [orders[half][k]])}, device_id_type=MESH)

    def forward(half, subset):
        for k in range(subset.bit_length(), steps):
            gather_copy(half, subset, k, False).start()

    def take(half, subset):
        k = subset.bit_length() - 1
        gather_copy(half, subset - (1 << k), k, True).wait_recv()

    for half in range(2):
        forward(half, 0)
    for d in range(1, n_ex):
        mask_copy(d, (me + n_ex - d) % n_ex).wait_recv()
    for copy in weights[1:]:
        copy.wait()

    def expert(owner):
        x = tokens[owner]
        logits = jnp.dot(x, router[...], preferred_element_type=F32)
        score = jax.nn.sigmoid(logits) * masks[owner].astype(F32)[:, 0:n_ex]
        total = jnp.sum(score, axis=1, keepdims=True)
        mine = jnp.sum(jnp.where(iota((padded, n_ex), 1) == me, score, 0.0), axis=1, keepdims=True)
        gate = mine / jnp.where(total == 0.0, 1.0, total)
        inner = jnp.maximum(jnp.dot(x, wg[...], preferred_element_type=F32), 0.0)
        inner = inner * jnp.dot(x, wu[...], preferred_element_type=F32)
        out = jnp.dot(inner.astype(BF16), wd[...], preferred_element_type=F32)
        partial[owner] = (out * gate).astype(BF16)

    def return_copy(half, subset, arriving):
        k = subset.bit_length() - 1
        start, size = spans[half]
        owner = flip(me, flips_of(half, subset))
        sem = half * n_ex + subset
        return pltpu.make_async_remote_copy(
            src_ref=partial.at[owner, pl.ds(start, size)], dst_ref=inbox.at[subset, pl.ds(start, size)],
            send_sem=r_s.at[sem], recv_sem=r_r.at[sem],
            device_id={"expert": flip(me, [orders[half][k]])}, device_id_type=MESH)

    def collect(half, subset):
        return_copy(half, subset, True).wait_recv()
        k = subset.bit_length() - 1
        target = subset - (1 << k)
        if target:
            start, size = spans[half]
            rows = pl.ds(start, size)
            owner = flip(me, flips_of(half, target))
            both = partial[owner, rows].astype(F32) + inbox[subset, rows].astype(F32)
            partial[owner, rows] = both.astype(BF16)

    core = bits[0]
    groups = [[b for b in bits[1:] if m * 2 & b] for m in range(n_ex // 2)]
    groups.sort(key=len)

    def ready(flips):
        for half in range(2):
            subset = place(half, flips)
            collect(half, subset + (1 << (steps - 1)))
            if subset.bit_length() == steps - 1:
                return_copy(half, subset, False).start()

    done = []
    for i, flips in enumerate(groups):
        for half in range(2):
            subset = place(half, flips)
            if subset:
                take(half, subset)
                forward(half, subset)
        for half in range(2):
            take(half, place(half, flips + [core]))
        far = flip(me, flips)

        def pair(j, carry):
            expert(far + j * (core - 2 * core * ((far // core) % 2)))
            return carry

        lax.fori_loop(0, 2, pair, 0)
        for half in range(2):
            return_copy(half, place(half, flips + [core]), False).start()
        if done:
            ready(done[-1])
        done.append(flips)
    ready(done[-1])
    for k in range(steps - 2, -1, -1):
        for half in range(2):
            for subset in range(1 << k, 2 << k):
                if k < steps - 2:
                    return_copy(half, subset, False).start()
        for half in range(2):
            for subset in range(1 << k, 2 << k):
                collect(half, subset)
    for half in range(2):
        start, size = spans[half]
        rows = pl.ds(start, size)
        total = partial[me, rows].astype(F32)
        for k in range(steps):
            total += inbox[1 << k, rows].astype(F32)
        keep = min(size, count - start)
        layer_out[start:start + keep, :] = (hidden[start:start + keep, :] + total[0:keep]).astype(BF16)

    for d in range(1, n_dp):
        from_row(dep_k.at[0], got_k, mk_s, mk_r, d).wait_recv()
        from_row(dep_v.at[0], got_v, mv_s, mv_r, d).wait_recv()
    fresh_line = iota((context, 1), 0) == last_len
    for got, fresh, moved in ((got_k, fresh_k, moved_k), (got_v, fresh_v, moved_v)):
        new = fresh[0:16, :].astype(F32)[DEC - 1:DEC, :]
        picked = jnp.zeros(got.shape[1:], F32)
        for i in range(n_dp):
            picked = jnp.where(destination[0, i] == row, got[i].astype(F32), picked)
        moved[0] = jnp.where(fresh_line, new, picked).astype(BF16)

    for d in range(1, n_dp):
        to_row(ask, asked, ask_s, ask_r, d).wait_send()
        reply(d, row).wait_send()
        to_row(dep_k.at[0], got_k, mk_s, mk_r, d).wait_send()
        to_row(dep_v.at[0], got_v, mv_s, mv_r, d).wait_send()
    for d in range(1, n_ex):
        mask_copy(d, me).wait_send()
    for half in range(2):
        for k in range(steps):
            for subset in range(1 << k):
                gather_copy(half, subset, k, False).wait_send()
        for subset in range(1, n_ex):
            return_copy(half, subset, False).wait_send()


def on_device(
    n_dp, n_ex,
    queries, fresh_keys, fresh_values, residual, norm_gain, out_weight, router_weight,
    gate_weight, up_weight, down_weight, expert_ids, paged_keys, paged_values,
    decode_table, prefill_table, decode_len, prefill_len, departing_keys, departing_values, destination,
):
    count, width = queries.shape
    padded = (count + 15) // 16 * 16
    hidden_units = gate_weight.shape[2]
    cache = departing_keys.shape[1:]
    vmem = pl.BlockSpec(memory_space=pltpu.VMEM)
    smem = pl.BlockSpec(memory_space=pltpu.SMEM)
    anywhere = pl.BlockSpec(memory_space=pl.ANY)
    dma = pltpu.SemaphoreType.DMA
    return pl.pallas_call(
        functools.partial(kernel, n_dp, n_ex),
        out_shape=(
            jax.ShapeDtypeStruct((count, width), BF16),
            jax.ShapeDtypeStruct(departing_keys.shape, BF16),
            jax.ShapeDtypeStruct(departing_values.shape, BF16),
        ),
        in_specs=[smem] * 5 + [vmem] * 11 + [anywhere] * 4,
        out_specs=(vmem, vmem, vmem),
        scratch_shapes=[
            pltpu.VMEM((width, width), BF16),
            pltpu.VMEM((width, hidden_units), BF16),
            pltpu.VMEM((width, hidden_units), BF16),
            pltpu.VMEM((hidden_units, width), BF16),
            pltpu.VMEM((count, width), F32),
            pltpu.VMEM((count, width), F32),
            pltpu.VMEM((n_ex, padded, HEAD), BF16),
            pltpu.VMEM((n_ex, padded, width), BF16),
            pltpu.VMEM((n_ex, padded, width), BF16),
            pltpu.VMEM((n_ex, padded, width), BF16),
            pltpu.VMEM((16, HEAD), BF16),
            pltpu.VMEM((n_dp, 32, HEAD), F32),
            pltpu.VMEM((n_dp, 16, HEAD), BF16),
            pltpu.VMEM((n_dp, 32, HEAD), F32),
            pltpu.VMEM((n_dp,) + cache, BF16),
            pltpu.VMEM((n_dp,) + cache, BF16),
            dma((4,)),
            dma((n_dp,)), dma((n_dp,)), dma((n_dp,)), dma((n_dp,)),
            dma((n_dp,)), dma((n_dp,)), dma((n_dp,)), dma((n_dp,)),
            dma((n_ex,)), dma((n_ex,)),
            dma((2 * n_ex,)), dma((2 * n_ex,)), dma((2 * n_ex,)), dma((2 * n_ex,)),
        ],
        compiler_params=pltpu.CompilerParams(
            collective_id=0, has_side_effects=True, vmem_limit_bytes=56 * 1024 * 1024
        ),
    )(
        decode_table, prefill_table, decode_len, prefill_len, destination,
        queries, fresh_keys, fresh_values, residual, norm_gain.reshape(1, width), router_weight,
        expert_ids, paged_keys, paged_values, departing_keys, departing_values,
        out_weight, gate_weight, up_weight, down_weight,
    )


def solution(mesh):
    both = ("dp", "expert")
    return jax.shard_map(
        functools.partial(on_device, mesh.shape["dp"], mesh.shape["expert"]),
        mesh=mesh,
        in_specs=(
            P(both, None), P(both, None), P(both, None), P(both, None),
            P(), P(), P(),
            P("expert", None, None), P("expert", None, None), P("expert", None, None),
            P(both, None),
            P(both, None, None), P(both, None, None),
            P(both, None), P(both, None), P(both, None), P(both),
            P(both, None, None), P(both, None, None),
            P("expert", None),
        ),
        out_specs=(P(both, None), P(both, None, None), P(both, None, None)),
        check_vma=False,
    )
```

time: 189 us -> 113 us (0.60)
  Pallas kernels: 0 us -> 102 us
  waiting for transfers between devices: 40.1 us -> 0 us
  local copies, waits for them, and re-layouts: 49.4 us -> 9.93 us
  blocking collectives: 35.1 us -> 0 us
  matrix products: 29.1 us -> 0 us
  between operations: 17.2 us -> 1.3 us
  other arithmetic: 12.3 us -> 0 us
  starting transfers between devices: 4.84 us -> 0 us
    pallas_call x0 -> x1, Pallas kernels: none -> 102 us  [on_device(): pl.pallas_call(functools.partial(kernel, n_dp, n_ex), out_shape=(jax.Shap...]
    all_to_all x1 -> x0, blocking collectives: 35.1 us -> none  [on_device(): lax.all_to_all(outgoing, 'expert', split_axis=0, concat_axis=0, tiled=True)]
    dot_general x14 -> x0, matrix products: 29.1 us -> none  [the longest x1 6.75 us: on_device(): jnp.einsum('scf,fd->scd', inner, down_weight[0], preferred_element_type=j...]
    all_to_all x1 -> x0, waiting for transfers between devices: 25.7 us -> none  [on_device(): lax.all_to_all(processed, 'expert', split_axis=0, concat_axis=0, tiled=True)]
    concatenate x15 -> x0, local copies, waits for them, and re-layouts: 20.2 us -> none  [the longest x2 8.59 us: on_device(): jnp.concatenate([resident_keys, take_keys], axis=0)]
    convert_element_type x6 -> x0, local copies, waits for them, and re-layouts: 14.1 us -> none  [the longest x2 7.23 us: page_lookup(): return jnp.einsum('...p,pk->...k', selector, pool_flat, preferred_element...]
    all_gather x2 -> x0, waiting for transfers between devices: 13 us -> none  [the longest x1 13 us: on_device(): lax.all_gather(departing_keys, 'dp', axis=0, tiled=True)]
    reduce_sum x6 -> x0, other arithmetic: 7.71 us -> none  [the longest x1 4.35 us: on_device(): mixture = jnp.sum(gates[:, :, None] * route_out.astype(jnp.float32), axis=1)]
  transfers between devices with their start and end apart: 3 -> 0, of which waited for: 2 -> 0; matrix products, arithmetic and copies ran while one was open for 27% -> 0% of each run, Pallas kernels for 0% -> 0%
where the time goes in v1:
time: 113 us
  Pallas kernels  102 us (90%)
  local copies, waits for them, and re-layouts  9.93 us (9%)
  between operations  1.3 us (1%)
    pallas_call x1, Pallas kernels, on_device(): pl.pallas_call(functools.partial(kernel, n_dp, n_ex), out_shape=(jax.Shap...  102 us
    unnamed x8, local copies, waits for them, and re-layouts  8.63 us

profile of v1, /device:TPU:0, one launch (start us, length us, event | category | flops | bytes accessed | tf_op | source)
XLA Modules:
  0.0 113.0 jit_solution(14438587001537027563)
XLA Ops:
  1.3 1.4 %copy.23.dec_table = s32[7,4]{1,0:T(8,128)} copy(s32[7,4]{0,1:T(4,128)} %param.33) | data formatting | bytes 224 | tf_op args[13]
  2.6 1.3 %reshape.9.gain = f32[1,1536]{1,0:T(1,128)} reshape(f32[1536]{0:T(1024)} %param.24) | data formatting | bytes 12288 | tf_op jit(solution)/shard_map/reshape | solution.py:409
  3.9 1.4 %copy.25.ids = s32[136,4]{1,0:T(8,128)} copy(s32[136,4]{0,1:T(4,128)} %param.30) | data formatting | bytes 4352 | tf_op args[10]
  5.3 1.7 %copy.24.router = bf16[1536,8]{1,0:T(8,128)(2,1)} copy(bf16[1536,8]{0,1:T(8,128)(2,1)} %param.26) | data formatting | bytes 49152 | tf_op args[6]
  7.0 101.8 %shard_map.211 = (bf16[136,1536]{1,0:T(8,128)(2,1)}, bf16[1,512,256]{2,1,0:T(8,128)(2,1)}, bf16[1,512,256]{2,1,0:T(8,128)(2,1)}) custom-call(s32[7,4]{1,0:T(8,128)} %copy.23.dec_table, s32[1,4]{1,0:T(1,128)} %pre_table.1, s32[1,8]{1,0:T(1,128)} %dec_len.1, s32[1]{0:T(128)S(6)} %copy.29.pre_len, s32[1,4]{1,0:T(1,128)} %destination.1, ...), custom_call_target="tpu_custom_call" | custom-call | tf_op jit(solution)/shard_map/pallas_call | solution.py:372
  108.8 0.0 copy-start
  108.8 1.8 %copy.30 = bf16[136,1536]{1,0:T(8,128)(2,1)} copy(bf16[136,1536]{1,0:T(8,128)(2,1)} %get-tuple-element.6) | data formatting | bytes 835584
  110.7 1.7 %copy.31 = bf16[1,512,256]{2,1,0:T(8,128)(2,1)} copy(bf16[1,512,256]{2,1,0:T(8,128)(2,1)} %get-tuple-element.7) | data formatting | bytes 524288
  112.3 0.0 copy-done
  112.3 0.7 copy.32
Async XLA Ops:
  108.8 3.5 %copy-start = (bf16[1,512,256]{2,1,0:T(8,128)(2,1)S(1)}, bf16[1,512,256]{2,1,0:T(8,128)(2,1)}, u32[]{:S(2)}) copy-start(bf16[1,512,256]{2,1,0:T(8,128)(2,1)} %get-tuple-element.8) | copy-start | bytes 786436

commit v2 on v1

--- a/solution.py
+++ b/solution.py
@@ -30,8 +30,8 @@
     out_w, gate_w, up_w, down_w,
     layer_out, moved_k, moved_v,
     wo, wg, wu, wd, hidden, attended, masks, tokens, partial, inbox,
-    ask, answer, asked, answered, got_k, got_v,
-    w_sem, ask_s, ask_r, ans_s, ans_r, mk_s, mk_r, mv_s, mv_r, msk_s, msk_r, g_s, g_r, r_s, r_r,
+    ask, answer, asked, answered, far_kv, near_out, near_in,
+    w_sem, ask_s, ask_r, ans_s, ans_r, far_s, far_r, near_s, near_r, msk_s, msk_r, g_s, g_r, r_s, r_r,
 ):
     row = lax.axis_index("dp")
     me = lax.axis_index("expert")
@@ -83,10 +83,11 @@
     for d in range(1, n_dp):
         to_row(ask, asked, ask_s, ask_r, d).start()
 
-    chose = jnp.zeros((count, HEAD), F32)
-    lane = iota((count, HEAD), 1)
-    for k in range(ids.shape[1]):
-        chose = jnp.where(ids[:, k:k + 1] == lane, 1.0, chose)
+    chose = jnp.zeros((HEAD, count), F32)
+    line = iota((HEAD, count), 0)
+    for k in range(ids.shape[0]):
+        chose = jnp.where(ids[k:k + 1, :] == line, 1.0, chose)
+    chose = jnp.transpose(chose)
     masks[me] = jnp.concatenate([chose, jnp.zeros((padded - count, HEAD), F32)], axis=0).astype(BF16)
 
     def mask_copy(d, slot):
@@ -96,21 +97,15 @@
 
     for d in range(1, n_ex):
         mask_copy(d, me).start()
-
-    for d in range(1, n_dp):
-        to_row(dep_k.at[0], got_k, mk_s, mk_r, d).start()
-        to_row(dep_v.at[0], got_v, mv_s, mv_r, d).start()
-    got_k[row] = dep_k[0]
-    got_v[row] = dep_v[0]
 
     small = iota((16, page), 0)
     spot = iota((16, page), 1)
     lens = jnp.zeros((16, page), jnp.int32)
-    tables = [jnp.full((16, page), -1, jnp.int32) for _ in range(dec_table.shape[1])]
+    tables = [jnp.full((16, page), -1, jnp.int32) for _ in range(dec_table.shape[0])]
     for s in range(DEC - 1):
         lens = jnp.where(small == s, dec_len[0, s], lens)
         for p in range(len(tables)):
-            tables[p] = jnp.where(small == s, dec_table[s, p], tables[p])
+            tables[p] = jnp.where(small == s, dec_table[p, s], tables[p])
     pieces = []
     for g in range(pool_pages):
         piece = jnp.zeros((16, page), F32)
@@ -208,7 +203,7 @@
     x = residual[...].astype(F32) + jnp.dot(attended[...].astype(BF16), wo[...], preferred_element_type=F32)
     hidden[...] = x
     variance = jnp.mean(x * x, axis=-1, keepdims=True)
-    normed = x * lax.rsqrt(variance + 1e-06) * gain[...]
+    normed = x * lax.rsqrt(variance + 1e-06) * gain[...][None, :]
     tokens[me] = jnp.concatenate([normed, jnp.zeros((padded - count, x.shape[1]), F32)], axis=0).astype(BF16)
 
     def flip(index, flips):
@@ -241,6 +236,36 @@
 
     for half in range(2):
         forward(half, 0)
+
+    halves = n_dp // 2
+    across = (row + halves) % n_dp
+    base, spot = row // halves * halves, row % halves
+    leaving = (dep_k, dep_v)
+
+    def far_copy(t):
+        return pltpu.make_async_remote_copy(
+            src_ref=leaving[t].at[0], dst_ref=far_kv.at[t], send_sem=far_s.at[t], recv_sem=far_r.at[t],
+            device_id={"dp": across}, device_id_type=MESH)
+
+    def near_copy(t, d, slot):
+        sem = t * halves + d
+        return pltpu.make_async_remote_copy(
+            src_ref=near_out.at[t, d], dst_ref=near_in.at[t, slot], send_sem=near_s.at[sem],
+            recv_sem=near_r.at[sem], device_id={"dp": base + (spot + d) % halves}, device_id_type=MESH)
+
+    def choose(t, target, other):
+        item = jnp.where(destination[0, across] == target, far_kv[t].astype(F32), other)
+        return jnp.where(destination[0, row] == target, leaving[t][0].astype(F32), item)
+
+    def hand_over(t):
+        far_copy(t).wait_recv()
+        for d in range(1, halves):
+            target = base + (spot + d) % halves
+            near_out[t, d] = choose(t, target, jnp.zeros((context, dep_k.shape[2]), F32)).astype(BF16)
+            near_copy(t, d, spot).start()
+
+    for t in range(2):
+        far_copy(t).start()
     for d in range(1, n_ex):
         mask_copy(d, (me + n_ex - d) % n_ex).wait_recv()
     for copy in weights[1:]:
@@ -248,7 +273,7 @@
 
     def expert(owner):
         x = tokens[owner]
-        logits = jnp.dot(x, router[...], preferred_element_type=F32)
+        logits = lax.dot_general(x, router[...], NT, preferred_element_type=F32)
         score = jax.nn.sigmoid(logits) * masks[owner].astype(F32)[:, 0:n_ex]
         total = jnp.sum(score, axis=1, keepdims=True)
         mine = jnp.sum(jnp.where(iota((padded, n_ex), 1) == me, score, 0.0), axis=1, keepdims=True)
@@ -311,7 +336,10 @@
         if done:
             ready(done[-1])
         done.append(flips)
+        if i == len(groups) - 2:
+            hand_over(0)
     ready(done[-1])
+    hand_over(1)
     for k in range(steps - 2, -1, -1):
         for half in range(2):
             for subset in range(1 << k, 2 << k):
@@ -329,22 +357,26 @@
         keep = min(size, count - start)
         layer_out[start:start + keep, :] = (hidden[start:start + keep, :] + total[0:keep]).astype(BF16)
 
-    for d in range(1, n_dp):
-        from_row(dep_k.at[0], got_k, mk_s, mk_r, d).wait_recv()
-        from_row(dep_v.at[0], got_v, mv_s, mv_r, d).wait_recv()
     fresh_line = iota((context, 1), 0) == last_len
-    for got, fresh, moved in ((got_k, fresh_k, moved_k), (got_v, fresh_v, moved_v)):
+    for t, (fresh, moved) in enumerate(((fresh_k, moved_k), (fresh_v, moved_v))):
         new = fresh[0:16, :].astype(F32)[DEC - 1:DEC, :]
-        picked = jnp.zeros(got.shape[1:], F32)
-        for i in range(n_dp):
-            picked = jnp.where(destination[0, i] == row, got[i].astype(F32), picked)
+        picked = jnp.zeros((context, dep_k.shape[2]), F32)
+        for d in range(1, halves):
+            slot = (spot + halves - d) % halves
+            near_copy(t, d, slot).wait_recv()
+            source = base + slot
+            due = (destination[0, source] == row) | (destination[0, (source + halves) % n_dp] == row)
+            picked = jnp.where(due, near_in[t, slot].astype(F32), picked)
+        picked = choose(t, row, picked)
         moved[0] = jnp.where(fresh_line, new, picked).astype(BF16)
 
     for d in range(1, n_dp):
         to_row(ask, asked, ask_s, ask_r, d).wait_send()
         reply(d, row).wait_send()
-        to_row(dep_k.at[0], got_k, mk_s, mk_r, d).wait_send()
-        to_row(dep_v.at[0], got_v, mv_s, mv_r, d).wait_send()
+    for t in range(2):
+        far_copy(t).wait_send()
+        for d in range(1, halves):
+            near_copy(t, d, spot).wait_send()
     for d in range(1, n_ex):
         mask_copy(d, me).wait_send()
     for half in range(2):
@@ -353,6 +385,11 @@
                 gather_copy(half, subset, k, False).wait_send()
         for subset in range(1, n_ex):
             return_copy(half, subset, False).wait_send()
+
+
+def write_out(*refs):
+    for src, dst in zip(refs[:3], refs[3:]):
+        dst[...] = src[...]
 
 
 def on_device(
@@ -369,7 +406,7 @@
     smem = pl.BlockSpec(memory_space=pltpu.SMEM)
     anywhere = pl.BlockSpec(memory_space=pl.ANY)
     dma = pltpu.SemaphoreType.DMA
-    return pl.pallas_call(
+    results = pl.pallas_call(
         functools.partial(kernel, n_dp, n_ex),
         out_shape=(
             jax.ShapeDtypeStruct((count, width), BF16),
@@ -393,11 +430,12 @@
             pltpu.VMEM((n_dp, 32, HEAD), F32),
             pltpu.VMEM((n_dp, 16, HEAD), BF16),
             pltpu.VMEM((n_dp, 32, HEAD), F32),
-            pltpu.VMEM((n_dp,) + cache, BF16),
-            pltpu.VMEM((n_dp,) + cache, BF16),
+            pltpu.VMEM((2,) + cache, BF16),
+            pltpu.VMEM((2, n_dp // 2) + cache, BF16),
+            pltpu.VMEM((2, n_dp // 2) + cache, BF16),
             dma((4,)),
             dma((n_dp,)), dma((n_dp,)), dma((n_dp,)), dma((n_dp,)),
-            dma((n_dp,)), dma((n_dp,)), dma((n_dp,)), dma((n_dp,)),
+            dma((2,)), dma((2,)), dma((n_dp,)), dma((n_dp,)),
             dma((n_ex,)), dma((n_ex,)),
             dma((2 * n_ex,)), dma((2 * n_ex,)), dma((2 * n_ex,)), dma((2 * n_ex,)),
         ],
@@ -405,11 +443,17 @@
             collective_id=0, has_side_effects=True, vmem_limit_bytes=56 * 1024 * 1024
         ),
     )(
-        decode_table, prefill_table, decode_len, prefill_len, destination,
-        queries, fresh_keys, fresh_values, residual, norm_gain.reshape(1, width), router_weight,
-        expert_ids, paged_keys, paged_values, departing_keys, departing_values,
+        decode_table.T, prefill_table, decode_len, prefill_len, destination,
+        queries, fresh_keys, fresh_values, residual, norm_gain, router_weight.T,
+        expert_ids.T, paged_keys, paged_values, departing_keys, departing_values,
         out_weight, gate_weight, up_weight, down_weight,
     )
+    return pl.pallas_call(
+        write_out,
+        out_shape=tuple(jax.ShapeDtypeStruct(x.shape, x.dtype) for x in results),
+        in_specs=[vmem] * 3,
+        out_specs=(vmem,) * 3,
+    )(*results)
 
 
 def solution(mesh):

time: 113 us -> 63.6 us (0.56)
  Pallas kernels: 102 us -> 62.1 us
  local copies, waits for them, and re-layouts: 9.93 us -> 0 us
    pallas_call x1, Pallas kernels: 102 us -> 60 us  [on_device(): pl.pallas_call(functools.partial(kernel, n_dp, n_ex), out_shape=(jax.Shap...]
    unnamed x8 -> x0, local copies, waits for them, and re-layouts: 8.63 us -> none
    pallas_call x0 -> x1, Pallas kernels: none -> 2.1 us  [on_device(): pl.pallas_call(write_out, out_shape=tuple((jax.ShapeDtypeStruct(x.shape,...]
    reshape x1 -> x0, local copies, waits for them, and re-layouts: 1.29 us -> none  [on_device(): norm_gain.reshape(1, width)]
where the time goes in v2:
time: 63.6 us; the launch traced here: 63.4 us
  Pallas kernels  62.1 us (98%)
  between operations  1.29 us (2%)
    pallas_call x1, Pallas kernels, on_device(): pl.pallas_call(functools.partial(kernel, n_dp, n_ex), out_shape=(jax.Shap...  60 us
    pallas_call x1, Pallas kernels, on_device(): pl.pallas_call(write_out, out_shape=tuple((jax.ShapeDtypeStruct(x.shape,...  2.1 us

profile of v2, /device:TPU:0, one launch (start us, length us, event | category | flops | bytes accessed | tf_op | source)
XLA Modules:
  0.0 63.4 jit_solution(12931978399269636559)
XLA Ops:
  1.3 60.0 %shard_map.211 = (bf16[136,1536]{1,0:T(8,128)(2,1)}, bf16[1,512,256]{2,1,0:T(8,128)(2,1)}, bf16[1,512,256]{2,1,0:T(8,128)(2,1)}) custom-call(s32[4,7]{1,0:T(4,128)} %bitcast.5, s32[1,4]{1,0:T(1,128)} %pre_table.1, s32[1,8]{1,0:T(1,128)} %dec_len.1, s32[1]{0:T(128)S(6)} %copy.23.pre_len, s32[1,4]{1,0:T(1,128)} %destination.1, bf16[136,1536]{1,0:T(8,128)(2,1)} %queries.1, ...), custom_call_target="tpu_custom_call" | custom-call | tf_op jit(solution)/shard_map/pallas_call | solution.py:409
  61.3 2.1 %shard_map.212 = (bf16[136,1536]{1,0:T(8,128)(2,1)}, bf16[1,512,256]{2,1,0:T(8,128)(2,1)}, bf16[1,512,256]{2,1,0:T(8,128)(2,1)}) custom-call(bf16[136,1536]{1,0:T(8,128)(2,1)} %get-tuple-element.6.refs_0_, bf16[1,512,256]{2,1,0:T(8,128)(2,1)} %get-tuple-element.7.refs_1_, bf16[1,512,256]{2,1,0:T(8,128)(2,1)} %get-tuple-element.8.refs_2_), custom_call_target="tpu_custom_call" | custom-call | tf_op jit(solution)/shard_map/pallas_call | solution.py:451

commit v3 on v2

--- a/solution.py
+++ b/solution.py
@@ -189,6 +189,36 @@
 
     for d in range(1, n_dp):
         reply(d, (row + n_dp - d) % n_dp).wait_recv()
+
+    halves = n_dp // 2
+    across = (row + halves) % n_dp
+    base, spot = row // halves * halves, row % halves
+    leaving = (dep_k, dep_v)
+
+    def far_copy(t):
+        return pltpu.make_async_remote_copy(
+            src_ref=leaving[t].at[0], dst_ref=far_kv.at[t], send_sem=far_s.at[t], recv_sem=far_r.at[t],
+            device_id={"dp": across}, device_id_type=MESH)
+
+    def near_copy(t, d, slot):
+        sem = t * halves + d
+        return pltpu.make_async_remote_copy(
+            src_ref=near_out.at[t, d], dst_ref=near_in.at[t, slot], send_sem=near_s.at[sem],
+            recv_sem=near_r.at[sem], device_id={"dp": base + (spot + d) % halves}, device_id_type=MESH)
+
+    def choose(t, target, other):
+        item = jnp.where(destination[0, across] == target, far_kv[t].astype(F32), other)
+        return jnp.where(destination[0, row] == target, leaving[t][0].astype(F32), item)
+
+    def hand_over(t):
+        far_copy(t).wait_recv()
+        for d in range(1, halves):
+            target = base + (spot + d) % halves
+            near_out[t, d] = choose(t, target, jnp.zeros((context, dep_k.shape[2]), F32)).astype(BF16)
+            near_copy(t, d, spot).start()
+
+    for t in range(2):
+        far_copy(t).start()
     arrived = jnp.zeros((32, HEAD), F32)
     for i in range(n_dp):
         arrived = jnp.where(destination[0, i] == row, answered[i], arrived)
@@ -234,38 +264,10 @@
         k = subset.bit_length() - 1
         gather_copy(half, subset - (1 << k), k, True).wait_recv()
 
-    for half in range(2):
-        forward(half, 0)
-
-    halves = n_dp // 2
-    across = (row + halves) % n_dp
-    base, spot = row // halves * halves, row % halves
-    leaving = (dep_k, dep_v)
-
-    def far_copy(t):
-        return pltpu.make_async_remote_copy(
-            src_ref=leaving[t].at[0], dst_ref=far_kv.at[t], send_sem=far_s.at[t], recv_sem=far_r.at[t],
-            device_id={"dp": across}, device_id_type=MESH)
-
-    def near_copy(t, d, slot):
-        sem = t * halves + d
-        return pltpu.make_async_remote_copy(
-            src_ref=near_out.at[t, d], dst_ref=near_in.at[t, slot], send_sem=near_s.at[sem],
-            recv_sem=near_r.at[sem], device_id={"dp": base + (spot + d) % halves}, device_id_type=MESH)
-
-    def choose(t, target, other):
-        item = jnp.where(destination[0, across] == target, far_kv[t].astype(F32), other)
-        return jnp.where(destination[0, row] == target, leaving[t][0].astype(F32), item)
-
-    def hand_over(t):
-        far_copy(t).wait_recv()
-        for d in range(1, halves):
-            target = base + (spot + d) % halves
-            near_out[t, d] = choose(t, target, jnp.zeros((context, dep_k.shape[2]), F32)).astype(BF16)
-            near_copy(t, d, spot).start()
-
-    for t in range(2):
-        far_copy(t).start()
+    for k in range(steps):
+        for half in range(2):
+            gather_copy(half, 0, k, False).start()
+
     for d in range(1, n_ex):
         mask_copy(d, (me + n_ex - d) % n_ex).wait_recv()
     for copy in weights[1:]:
@@ -322,11 +324,14 @@
             if subset:
                 take(half, subset)
                 forward(half, subset)
-        for half in range(2):
-            take(half, place(half, flips + [core]))
         far = flip(me, flips)
 
         def pair(j, carry):
+            @pl.when(j == 1)
+            def _():
+                for half in range(2):
+                    take(half, place(half, flips + [core]))
+
             expert(far + j * (core - 2 * core * ((far // core) % 2)))
             return carry
 

time: 63.6 us -> 62.8 us (0.987)
  Pallas kernels: 62.1 us -> 61.3 us
    pallas_call x1, Pallas kernels: 60 us -> 59.2 us  [on_device(): pl.pallas_call(functools.partial(kernel, n_dp, n_ex), out_shape=(jax.Shap...]
where the time goes in v3:
time: 62.8 us; the launch traced here: 62.6 us
  Pallas kernels  61.3 us (98%)
  between operations  1.29 us (2%)
    pallas_call x1, Pallas kernels, on_device(): pl.pallas_call(functools.partial(kernel, n_dp, n_ex), out_shape=(jax.Shap...  59.2 us
    pallas_call x1, Pallas kernels, on_device(): pl.pallas_call(write_out, out_shape=tuple((jax.ShapeDtypeStruct(x.shape,...  2.1 us

profile of v3, /device:TPU:0, one launch (start us, length us, event | category | flops | bytes accessed | tf_op | source)
XLA Modules:
  0.0 62.6 jit_solution(5552079525637691045)
XLA Ops:
  1.3 59.2 %shard_map.211 = (bf16[136,1536]{1,0:T(8,128)(2,1)}, bf16[1,512,256]{2,1,0:T(8,128)(2,1)}, bf16[1,512,256]{2,1,0:T(8,128)(2,1)}) custom-call(s32[4,7]{1,0:T(4,128)} %bitcast.5, s32[1,4]{1,0:T(1,128)} %pre_table.1, s32[1,8]{1,0:T(1,128)} %dec_len.1, s32[1]{0:T(128)S(6)} %copy.23.pre_len, s32[1,4]{1,0:T(1,128)} %destination.1, bf16[136,1536]{1,0:T(8,128)(2,1)} %queries.1, ...), custom_call_target="tpu_custom_call" | custom-call | tf_op jit(solution)/shard_map/pallas_call | solution.py:414
  60.5 2.1 %shard_map.212 = (bf16[136,1536]{1,0:T(8,128)(2,1)}, bf16[1,512,256]{2,1,0:T(8,128)(2,1)}, bf16[1,512,256]{2,1,0:T(8,128)(2,1)}) custom-call(bf16[136,1536]{1,0:T(8,128)(2,1)} %get-tuple-element.6.refs_0_, bf16[1,512,256]{2,1,0:T(8,128)(2,1)} %get-tuple-element.7.refs_1_, bf16[1,512,256]{2,1,0:T(8,128)(2,1)} %get-tuple-element.8.refs_2_), custom_call_target="tpu_custom_call" | custom-call | tf_op jit(solution)/shard_map/pallas_call | solution.py:456
